TPU v7x, 32 devices: a whole 2x2x4 slice. The times are simulated.
32 devices in a mesh: fibre: 16 (over z, x, core), freq: 2 (over y).
Axes of the slice: x: 2, y: 2, z: 4, core: 2. Of those that a mesh axis runs over, the one named last changes fastest.
Arguments:
- traces: bfloat16 [2, 1024, 4096], P(None, 'fibre'), may hold values from -50 to 50, as said below
- live: int32 [1024], P('fibre'), may hold values 0 or 1
- reach: int32 [16], P('fibre'), may hold values from 1 to 8
Outputs:
- correlations: float32 [16, 8, 64, 64, 128], P('fibre', 'freq')
Inputs may be any that keep to these rules, and one draw needn't show every extreme that they name: `traces`: records of the fibre's channels.
All inputs are finite; a program needn't handle non-finite values. No bound on the sum of `live` on one device may be relied on, other than what follows from the above.
Results may differ from a plain program's by a relative error of at most 0.0057.
Values may be sent and summed in bfloat16 or wider, within the bound.
No kernel may reach another device: no remote copies, remote signals or barrier semaphores. Data moves between devices by JAX's collectives and lax.ppermute only.
A program may use at most 64 MiB of HBM per device.

v0:
```python
import math

import jax
import jax.numpy as jnp
from jax import lax
from jax.sharding import PartitionSpec as P

BAND = 64
OFF = 8
LAGS = 128


def from_behind(x, axis, by):
    peers = lax.axis_size(axis)
    pairs = [(i, i + by) for i in range(peers) if 0 <= i + by < peers]
    return lax.ppermute(x, axis, pairs)


def phase_angle(freq_ids, sample_ids, period):
    product = freq_ids[:, None] * sample_ids[None, :] % period
    return product.astype(jnp.float32) * (2.0 * math.pi / period)


def correlate(own_block, partner, first_freq, windows, channels, samples):
    freq_span = own_block.shape[2]
    block_width = math.gcd(freq_span, 256)
    own_split = own_block.reshape(2, windows, channels, freq_span)
    partner_split = partner.reshape(2, windows, channels, freq_span)
    lag_steps = jnp.arange(LAGS, dtype=jnp.int32) - LAGS // 2 + samples

    def accumulate(block_index, summed):
        first = block_index * block_width
        own_part = lax.dynamic_slice_in_dim(own_split, first, block_width, 3).astype(jnp.float32)
        partner_part = lax.dynamic_slice_in_dim(partner_split, first, block_width, 3).astype(
            jnp.float32
        )
        cross_real = (
            own_part[0][:, :, None, :] * partner_part[0][:, None, :, :]
            + own_part[1][:, :, None, :] * partner_part[1][:, None, :, :]
        ).sum(0)
        cross_imag = (
            own_part[1][:, :, None, :] * partner_part[0][:, None, :, :]
            - own_part[0][:, :, None, :] * partner_part[1][:, None, :, :]
        ).sum(0)
        cross_block = (
            jnp.stack([cross_real, cross_imag], axis=2)
            .astype(jnp.bfloat16)
            .reshape(channels * channels, 2 * block_width)
        )
        freq_ids = first_freq + first + jnp.arange(block_width, dtype=jnp.int32)
        angles = phase_angle(freq_ids, lag_steps, samples)
        lag_table = jnp.concatenate(
            [jnp.cos(angles).astype(jnp.bfloat16), (-jnp.sin(angles)).astype(jnp.bfloat16)]
        )
        return summed + jnp.dot(cross_block, lag_table, preferred_element_type=jnp.float32).reshape(
            channels, channels, LAGS
        )

    start_value = jnp.zeros((channels, channels, LAGS), jnp.float32)
    return lax.fori_loop(0, freq_span // block_width, accumulate, start_value)


def whiten_range(flat_rows, live, first_freq, span, windows, samples):
    row_count = flat_rows.shape[0]
    dft_width = math.gcd(span, 128)
    sample_ids = jnp.arange(samples, dtype=jnp.int32)

    def transform(block_index):
        freq_ids = first_freq + block_index * dft_width + jnp.arange(dft_width, dtype=jnp.int32)
        angles = phase_angle(freq_ids, sample_ids, samples)
        cosine = jnp.cos(angles).astype(jnp.bfloat16)
        sine_table = (-jnp.sin(angles)).astype(jnp.bfloat16)
        real_part = lax.dot_general(
            flat_rows, cosine, (((1,), (1,)), ((), ())), preferred_element_type=jnp.float32
        )
        imag_part = lax.dot_general(
            flat_rows, sine_table, (((1,), (1,)), ((), ())), preferred_element_type=jnp.float32
        )
        return jnp.stack([real_part, imag_part])

    blocks = lax.map(transform, jnp.arange(span // dft_width, dtype=jnp.int32))
    spectra = blocks.transpose(1, 2, 0, 3).reshape(2, row_count, span)
    band_power = (
        (spectra[0] * spectra[0] + spectra[1] * spectra[1])
        .reshape(row_count, span // BAND, BAND)
        .mean(-1)
    )
    whiten_gain = jnp.repeat(1.0 / jnp.sqrt(band_power + 1e-06), BAND, axis=1)
    alive_rows = jnp.tile(live.astype(jnp.float32), windows)
    return (spectra * whiten_gain[None] * alive_rows[None, :, None]).astype(jnp.bfloat16)


def per_device(traces, live, reach):
    windows, channels, samples = traces.shape
    row_count = windows * channels
    freq_count = samples // 2
    freq_groups = lax.axis_size("freq")
    local_freqs = freq_count // freq_groups
    band_index = lax.axis_index("freq")
    flat_rows = traces.reshape(row_count, samples)
    owned_offsets = OFF // freq_groups
    whitened = whiten_range(
        flat_rows, live, band_index * local_freqs, local_freqs, windows, samples
    )
    partners = whitened[None]
    filled = 1
    while filled < OFF:
        arrived = from_behind(partners, "fibre", -filled)
        partners = jnp.concatenate([partners, arrived])
        filled = filled * 2
    own_whole = lax.all_gather(whitened, "freq", axis=2, tiled=True)
    my_partners = lax.all_to_all(partners, "freq", split_axis=0, concat_axis=3, tiled=True)
    result = lax.map(
        lambda partner: correlate(own_whole, partner, 0, windows, channels, samples), my_partners
    )
    offset_ids = band_index * owned_offsets + jnp.arange(owned_offsets, dtype=jnp.int32)
    keep_mask = (offset_ids < reach[0]).astype(jnp.float32)
    normal_scale = 1.0 / math.sqrt(windows * freq_count)
    return (result * normal_scale * keep_mask[:, None, None, None])[None]


def solution(mesh):
    placed = (P(None, "fibre", None), P("fibre"), P("fibre"))
    return jax.shard_map(
        per_device,
        mesh=mesh,
        in_specs=placed,
        out_specs=P("fibre", "freq", None, None, None),
        check_vma=False,
    )
```

profile of v0, /device:TPU:21, one launch (start us, length us, event | category | flops | bytes accessed | tf_op | source)
XLA Modules:
  0.0 744.6 jit_solution(10201174978579751794)
XLA Ops:
  6.5 149.2 %while.58 = (s32[]{:T(128)}, f32[8,2,128,128]{2,3,0,1:T(8,128)S(1)}, s32[8]{0:T(128)S(1)}, s32[]{:T(128)}, bf16[128,4096]{1,0:T(8,128)(2,1)}, /*index=5*/s32[]{:T(128)}, s32[1]{0:T(128)}) while((s32[]{:T(128)}, f32[8,2,128,128]{2,3,0,1:T(8,128)S(1)}, s32[8]{0:T(128)S(1)}, s32[]{:T(128)}, bf16[128,4096]{1,0:T(8,128)(2,1)}, ...), condition=%wide.region_1.2_spmd.clone, body=%wide.region_0.1_spmd.clone.sunk | while | flops 284721280 | bytes 6686357 | solution.py:81
  7.8 9.3 %convolution_bitcast_fusion.4 = f32[1,128,128]{1,2,0:T(8,128)S(1)} fusion(bf16[128,4096]{1,0:T(8,128)(2,1)} %get-tuple-element.558, s32[128]{0:T(128)S(1)} %iota_add_fusion.6), kind=kOutput, calls=%fused_computation.14.clone.1 | convolution fusion | flops 142606336 | bytes 1114624 | tf_op jit(solution)/shard_map/while/body/eval_jaxpr/dot_general | solution.py:76
  17.2 7.9 %convolution_bitcast_fusion.5 = f32[1,128,128]{1,2,0:T(8,128)S(1)} fusion(bf16[128,4096]{1,0:T(8,128)(2,1)S(1)} %copy-done.1, s32[128]{0:T(128)S(1)} %iota_add_fusion.6), kind=kOutput, calls=%fused_computation.15.clone.1 | convolution fusion | flops 142082048 | bytes 1114624 | tf_op jit(solution)/shard_map/while/body/eval_jaxpr/dot_general | solution.py:73
  26.5 9.3 %convolution_bitcast_fusion.4 = f32[1,128,128]{1,2,0:T(8,128)S(1)} fusion(bf16[128,4096]{1,0:T(8,128)(2,1)} %get-tuple-element.558, s32[128]{0:T(128)S(1)} %iota_add_fusion.6), kind=kOutput, calls=%fused_computation.14.clone.1 | convolution fusion | flops 142606336 | bytes 1114624 | tf_op jit(solution)/shard_map/while/body/eval_jaxpr/dot_general | solution.py:76
  35.8 7.9 %convolution_bitcast_fusion.5 = f32[1,128,128]{1,2,0:T(8,128)S(1)} fusion(bf16[128,4096]{1,0:T(8,128)(2,1)S(1)} %copy-done.1, s32[128]{0:T(128)S(1)} %iota_add_fusion.6), kind=kOutput, calls=%fused_computation.15.clone.1 | convolution fusion | flops 142082048 | bytes 1114624 | tf_op jit(solution)/shard_map/while/body/eval_jaxpr/dot_general | solution.py:73
  45.1 9.3 %convolution_bitcast_fusion.4 = f32[1,128,128]{1,2,0:T(8,128)S(1)} fusion(bf16[128,4096]{1,0:T(8,128)(2,1)} %get-tuple-element.558, s32[128]{0:T(128)S(1)} %iota_add_fusion.6), kind=kOutput, calls=%fused_computation.14.clone.1 | convolution fusion | flops 142606336 | bytes 1114624 | tf_op jit(solution)/shard_map/while/body/eval_jaxpr/dot_general | solution.py:76
  54.5 7.9 %convolution_bitcast_fusion.5 = f32[1,128,128]{1,2,0:T(8,128)S(1)} fusion(bf16[128,4096]{1,0:T(8,128)(2,1)S(1)} %copy-done.1, s32[128]{0:T(128)S(1)} %iota_add_fusion.6), kind=kOutput, calls=%fused_computation.15.clone.1 | convolution fusion | flops 142082048 | bytes 1114624 | tf_op jit(solution)/shard_map/while/body/eval_jaxpr/dot_general | solution.py:73
  63.7 9.3 %convolution_bitcast_fusion.4 = f32[1,128,128]{1,2,0:T(8,128)S(1)} fusion(bf16[128,4096]{1,0:T(8,128)(2,1)} %get-tuple-element.558, s32[128]{0:T(128)S(1)} %iota_add_fusion.6), kind=kOutput, calls=%fused_computation.14.clone.1 | convolution fusion | flops 142606336 | bytes 1114624 | tf_op jit(solution)/shard_map/while/body/eval_jaxpr/dot_general | solution.py:76
  73.1 7.9 %convolution_bitcast_fusion.5 = f32[1,128,128]{1,2,0:T(8,128)S(1)} fusion(bf16[128,4096]{1,0:T(8,128)(2,1)S(1)} %copy-done.1, s32[128]{0:T(128)S(1)} %iota_add_fusion.6), kind=kOutput, calls=%fused_computation.15.clone.1 | convolution fusion | flops 142082048 | bytes 1114624 | tf_op jit(solution)/shard_map/while/body/eval_jaxpr/dot_general | solution.py:73
  82.3 9.3 %convolution_bitcast_fusion.4 = f32[1,128,128]{1,2,0:T(8,128)S(1)} fusion(bf16[128,4096]{1,0:T(8,128)(2,1)} %get-tuple-element.558, s32[128]{0:T(128)S(1)} %iota_add_fusion.6), kind=kOutput, calls=%fused_computation.14.clone.1 | convolution fusion | flops 142606336 | bytes 1114624 | tf_op jit(solution)/shard_map/while/body/eval_jaxpr/dot_general | solution.py:76
  91.7 7.9 %convolution_bitcast_fusion.5 = f32[1,128,128]{1,2,0:T(8,128)S(1)} fusion(bf16[128,4096]{1,0:T(8,128)(2,1)S(1)} %copy-done.1, s32[128]{0:T(128)S(1)} %iota_add_fusion.6), kind=kOutput, calls=%fused_computation.15.clone.1 | convolution fusion | flops 142082048 | bytes 1114624 | tf_op jit(solution)/shard_map/while/body/eval_jaxpr/dot_general | solution.py:73
  101.0 9.3 %convolution_bitcast_fusion.4 = f32[1,128,128]{1,2,0:T(8,128)S(1)} fusion(bf16[128,4096]{1,0:T(8,128)(2,1)} %get-tuple-element.558, s32[128]{0:T(128)S(1)} %iota_add_fusion.6), kind=kOutput, calls=%fused_computation.14.clone.1 | convolution fusion | flops 142606336 | bytes 1114624 | tf_op jit(solution)/shard_map/while/body/eval_jaxpr/dot_general | solution.py:76
  110.3 7.9 %convolution_bitcast_fusion.5 = f32[1,128,128]{1,2,0:T(8,128)S(1)} fusion(bf16[128,4096]{1,0:T(8,128)(2,1)S(1)} %copy-done.1, s32[128]{0:T(128)S(1)} %iota_add_fusion.6), kind=kOutput, calls=%fused_computation.15.clone.1 | convolution fusion | flops 142082048 | bytes 1114624 | tf_op jit(solution)/shard_map/while/body/eval_jaxpr/dot_general | solution.py:73
  119.6 9.3 %convolution_bitcast_fusion.4 = f32[1,128,128]{1,2,0:T(8,128)S(1)} fusion(bf16[128,4096]{1,0:T(8,128)(2,1)} %get-tuple-element.558, s32[128]{0:T(128)S(1)} %iota_add_fusion.6), kind=kOutput, calls=%fused_computation.14.clone.1 | convolution fusion | flops 142606336 | bytes 1114624 | tf_op jit(solution)/shard_map/while/body/eval_jaxpr/dot_general | solution.py:76
  128.9 7.9 %convolution_bitcast_fusion.5 = f32[1,128,128]{1,2,0:T(8,128)S(1)} fusion(bf16[128,4096]{1,0:T(8,128)(2,1)S(1)} %copy-done.1, s32[128]{0:T(128)S(1)} %iota_add_fusion.6), kind=kOutput, calls=%fused_computation.15.clone.1 | convolution fusion | flops 142082048 | bytes 1114624 | tf_op jit(solution)/shard_map/while/body/eval_jaxpr/dot_general | solution.py:73
  138.2 9.3 %convolution_bitcast_fusion.4 = f32[1,128,128]{1,2,0:T(8,128)S(1)} fusion(bf16[128,4096]{1,0:T(8,128)(2,1)} %get-tuple-element.558, s32[128]{0:T(128)S(1)} %iota_add_fusion.6), kind=kOutput, calls=%fused_computation.14.clone.1 | convolution fusion | flops 142606336 | bytes 1114624 | tf_op jit(solution)/shard_map/while/body/eval_jaxpr/dot_general | solution.py:76
  147.6 7.9 %convolution_bitcast_fusion.5 = f32[1,128,128]{1,2,0:T(8,128)S(1)} fusion(bf16[128,4096]{1,0:T(8,128)(2,1)S(1)} %copy-done.1, s32[128]{0:T(128)S(1)} %iota_add_fusion.6), kind=kOutput, calls=%fused_computation.15.clone.1 | convolution fusion | flops 142082048 | bytes 1114624 | tf_op jit(solution)/shard_map/while/body/eval_jaxpr/dot_general | solution.py:73
  159.2 7.9 %collective-permute-done = bf16[1,2,128,1024]{2,3,1,0:T(8,128)(2,1)S(1)} collective-permute-done((bf16[1,2,128,1024]{2,3,1,0:T(8,128)(2,1)S(1)}, bf16[1,2,128,1024]{2,3,1,0:T(8,128)(2,1)S(1)}, u32[]{:S(2)}, u32[]{:S(2)}) %collective-permute-start) | collective-permute-done | bytes 524320 | tf_op jit(solution)/shard_map/ppermute | solution.py:16
  171.1 22.9 %collective-permute-done.1 = bf16[2,2,128,1024]{2,3,1,0:T(8,128)(2,1)S(1)} collective-permute-done((bf16[2,2,128,1024]{2,3,1,0:T(8,128)(2,1)S(1)}, bf16[2,2,128,1024]{2,3,1,0:T(8,128)(2,1)S(1)}, u32[]{:S(2)}, u32[]{:S(2)}) %collective-permute-start.1) | collective-permute-done | bytes 1048608 | tf_op jit(solution)/shard_map/ppermute | solution.py:16
  196.3 46.9 %collective-permute-done.2 = bf16[4,2,128,1024]{2,3,1,0:T(8,128)(2,1)S(1)} collective-permute-done((bf16[4,2,128,1024]{2,3,1,0:T(8,128)(2,1)S(1)}, bf16[4,2,128,1024]{2,3,1,0:T(8,128)(2,1)S(1)}, u32[]{:S(2)}, u32[]{:S(2)}) %collective-permute-start.2) | collective-permute-done | bytes 2097184 | tf_op jit(solution)/shard_map/ppermute | solution.py:16
  245.4 5.8 all-to-all-start
  253.4 31.8 %all-gather.2.cloned.1.call-done = bf16[2,128,2048]{1,2,0:T(8,128)(2,1)} async-done(((bf16[2,128,1024]{1,2,0:T(8,128)(2,1)}), bf16[2,128,2048]{1,2,0:T(8,128)(2,1)}) %all-gather.2.cloned.1.call-update) | async-done | bytes 1048592 | tf_op jit(solution)/shard_map/all_gather | solution.py:111
  287.6 20.3 %all-to-all-done = bf16[8,2,128,1024]{2,3,1,0:T(8,128)(2,1)} async-done(((bf16[8,2,128,1024]{2,3,1,0:T(8,128)(2,1)}), bf16[8,2,128,1024]{2,3,1,0:T(8,128)(2,1)}, u32[]{:S(2)}, u32[]{:S(2)}) %all-to-all-start) | async-done | bytes 4194336 | tf_op jit(solution)/shard_map/all_to_all | solution.py:112
  312.4 416.7 %while.57 = (s32[]{:T(128)}, f32[4,64,64,128]{3,2,1,0:T(8,128)}, bf16[2,128,2048]{2,1,0:T(8,128)(2,1)}, bf16[4,2,128,2048]{2,3,1,0:T(8,128)(2,1)}, s32[]{:T(128)...) while((s32[]{:T(128)}, f32[4,64,64,128]{3,2,1,0:T(8,128)}, ...), condition=%wide.region_8.9_spmd, body=%wide.region_3.8_spmd.sunk | while | flops 555647360 | bytes 40374084 | solution.py:113
  314.2 100.8 %while.59 = (s32[]{:T(128)}, f32[64,64,128]{2,1,0:T(8,128)S(1)}, bf16[2,2,64,2048]{3,2,1,0:T(8,128)(2,1)}, bf16[2,2,64,2048]{3,2,1,0:T(8,128)(2,1)S(1)}, s32[]{:T(128)}, /*index=5*/s32[]{:T(128)}, s32[]{:T(128)}, s32[]{:T(128)}) while((s32[]{:T(128)}, f32[64,64,128]{2,1,0:T(8,128)S(1)}, bf16[2,2,64,2048]{3,2,1,0:T(8,128)(2,1)}, ...), condition=%wide.region_7.7_spmd.clone, body=%wide.region_4.6_spmd.clone.sunk | while | flops 555647360 | bytes 31984788 | solution.py:60
  315.3 4.6 add_reduce_fusion.2
  327.9 4.6 add_reduce_fusion.2
  340.5 4.6 add_reduce_fusion.2
  353.1 4.6 add_reduce_fusion.2
  365.7 4.6 add_reduce_fusion.2
  378.3 4.6 add_reduce_fusion.2
  390.9 4.6 add_reduce_fusion.2
  403.5 4.6 add_reduce_fusion.2
  418.4 100.8 %while.59 = (s32[]{:T(128)}, f32[64,64,128]{2,1,0:T(8,128)S(1)}, bf16[2,2,64,2048]{3,2,1,0:T(8,128)(2,1)}, bf16[2,2,64,2048]{3,2,1,0:T(8,128)(2,1)S(1)}, s32[]{:T(128)}, /*index=5*/s32[]{:T(128)}, s32[]{:T(128)}, s32[]{:T(128)}) while((s32[]{:T(128)}, f32[64,64,128]{2,1,0:T(8,128)S(1)}, bf16[2,2,64,2048]{3,2,1,0:T(8,128)(2,1)}, ...), condition=%wide.region_7.7_spmd.clone, body=%wide.region_4.6_spmd.clone.sunk | while | flops 555647360 | bytes 31984788 | solution.py:60
  419.4 4.6 add_reduce_fusion.2
  432.0 4.6 add_reduce_fusion.2
  507.7 4.6 add_reduce_fusion.2
  522.6 100.9 %while.59 = (s32[]{:T(128)}, f32[64,64,128]{2,1,0:T(8,128)S(1)}, bf16[2,2,64,2048]{3,2,1,0:T(8,128)(2,1)}, bf16[2,2,64,2048]{3,2,1,0:T(8,128)(2,1)S(1)}, s32[]{:T(128)}, /*index=5*/s32[]{:T(128)}, s32[]{:T(128)}, s32[]{:T(128)}) while((s32[]{:T(128)}, f32[64,64,128]{2,1,0:T(8,128)S(1)}, bf16[2,2,64,2048]{3,2,1,0:T(8,128)(2,1)}, ...), condition=%wide.region_7.7_spmd.clone, body=%wide.region_4.6_spmd.clone.sunk | while | flops 555647360 | bytes 31984788 | solution.py:60
  523.6 4.6 add_reduce_fusion.2
  548.8 4.6 add_reduce_fusion.2
  574.0 4.6 add_reduce_fusion.2
  611.8 4.6 add_reduce_fusion.2
  626.7 100.9 %while.59 = (s32[]{:T(128)}, f32[64,64,128]{2,1,0:T(8,128)S(1)}, bf16[2,2,64,2048]{3,2,1,0:T(8,128)(2,1)}, bf16[2,2,64,2048]{3,2,1,0:T(8,128)(2,1)S(1)}, s32[]{:T(128)}, /*index=5*/s32[]{:T(128)}, s32[]{:T(128)}, s32[]{:T(128)}) while((s32[]{:T(128)}, f32[64,64,128]{2,1,0:T(8,128)S(1)}, bf16[2,2,64,2048]{3,2,1,0:T(8,128)(2,1)}, ...), condition=%wide.region_7.7_spmd.clone, body=%wide.region_4.6_spmd.clone.sunk | while | flops 555647360 | bytes 31984788 | solution.py:60
  627.7 4.6 add_reduce_fusion.2
  653.0 4.6 add_reduce_fusion.2
  678.2 4.6 add_reduce_fusion.2
  716.0 4.6 add_reduce_fusion.2
  729.0 8.7 %multiply_bitcast_fusion = f32[1,4,64,64,128]{4,3,2,1,0:T(8,128)} fusion(f32[4,64,64,128]{3,2,1,0:T(8,128)} %get-tuple-element.326, f32[4]{0:T(128)S(1)} %copy-done), kind=kLoop, calls=%fused_computation.57 | loop fusion | flops 2097152 | bytes 16777232 | tf_op jit(solution)/shard_map/broadcast_in_dim | solution.py:119
  (384 shorter events, 353.2 us)
Async XLA Ops:
  7.8 9.4 %copy-start.1 = (bf16[128,4096]{1,0:T(8,128)(2,1)S(1)}, bf16[128,4096]{1,0:T(8,128)(2,1)}, u32[]{:S(2)}) copy-start(bf16[128,4096]{1,0:T(8,128)(2,1)} %get-tuple-element.558) | copy-start | bytes 3145732 | tf_op jit(solution)/shard_map/while
  26.5 9.4 %copy-start.1 = (bf16[128,4096]{1,0:T(8,128)(2,1)S(1)}, bf16[128,4096]{1,0:T(8,128)(2,1)}, u32[]{:S(2)}) copy-start(bf16[128,4096]{1,0:T(8,128)(2,1)} %get-tuple-element.558) | copy-start | bytes 3145732 | tf_op jit(solution)/shard_map/while
  45.1 9.4 %copy-start.1 = (bf16[128,4096]{1,0:T(8,128)(2,1)S(1)}, bf16[128,4096]{1,0:T(8,128)(2,1)}, u32[]{:S(2)}) copy-start(bf16[128,4096]{1,0:T(8,128)(2,1)} %get-tuple-element.558) | copy-start | bytes 3145732 | tf_op jit(solution)/shard_map/while
  63.7 9.4 %copy-start.1 = (bf16[128,4096]{1,0:T(8,128)(2,1)S(1)}, bf16[128,4096]{1,0:T(8,128)(2,1)}, u32[]{:S(2)}) copy-start(bf16[128,4096]{1,0:T(8,128)(2,1)} %get-tuple-element.558) | copy-start | bytes 3145732 | tf_op jit(solution)/shard_map/while
  82.3 9.4 %copy-start.1 = (bf16[128,4096]{1,0:T(8,128)(2,1)S(1)}, bf16[128,4096]{1,0:T(8,128)(2,1)}, u32[]{:S(2)}) copy-start(bf16[128,4096]{1,0:T(8,128)(2,1)} %get-tuple-element.558) | copy-start | bytes 3145732 | tf_op jit(solution)/shard_map/while
  100.9 9.4 %copy-start.1 = (bf16[128,4096]{1,0:T(8,128)(2,1)S(1)}, bf16[128,4096]{1,0:T(8,128)(2,1)}, u32[]{:S(2)}) copy-start(bf16[128,4096]{1,0:T(8,128)(2,1)} %get-tuple-element.558) | copy-start | bytes 3145732 | tf_op jit(solution)/shard_map/while
  119.6 9.4 %copy-start.1 = (bf16[128,4096]{1,0:T(8,128)(2,1)S(1)}, bf16[128,4096]{1,0:T(8,128)(2,1)}, u32[]{:S(2)}) copy-start(bf16[128,4096]{1,0:T(8,128)(2,1)} %get-tuple-element.558) | copy-start | bytes 3145732 | tf_op jit(solution)/shard_map/while
  138.2 9.4 %copy-start.1 = (bf16[128,4096]{1,0:T(8,128)(2,1)S(1)}, bf16[128,4096]{1,0:T(8,128)(2,1)}, u32[]{:S(2)}) copy-start(bf16[128,4096]{1,0:T(8,128)(2,1)} %get-tuple-element.558) | copy-start | bytes 3145732 | tf_op jit(solution)/shard_map/while
  155.7 0.7 copy-start.2
  156.6 10.5 %collective-permute-start = (bf16[1,2,128,1024]{2,3,1,0:T(8,128)(2,1)S(1)}, bf16[1,2,128,1024]{2,3,1,0:T(8,128)(2,1)S(1)}, u32[]{:S(2)}, u32[]{:S(2)}) collective-permute-start(bf16[1,2,128,1024]{2,3,1,0:T(8,128)(2,1)S(1)} %fusion.28), channel_id=1, source_target_pairs={{2,0},{4,2},{6,4},{8,6},{10,8},{12,10},{14,12},{16,14},{18,16},{20... | collective-permute-start | bytes 1572872 | tf_op jit(solution)/shard_map/ppermute | solution.py:16
  167.3 26.8 %collective-permute-start.1 = (bf16[2,2,128,1024]{2,3,1,0:T(8,128)(2,1)S(1)}, bf16[2,2,128,1024]{2,3,1,0:T(8,128)(2,1)S(1)}, u32[]{:S(2)}, u32[]{:S(2)}) collective-permute-start(bf16[2,2,128,1024]{2,3,1,0:T(8,128)(2,1)S(1)} %pad_maximum_fusion.2), channel_id=1, source_target_pairs={{4,0},{6,2},{8,4},{10,6},{12,8},{14,10},{16,12},{18,14},{20,16},{2... | collective-permute-start | bytes 3145736 | tf_op jit(solution)/shard_map/ppermute | solution.py:16
  194.2 49.0 %collective-permute-start.2 = (bf16[4,2,128,1024]{2,3,1,0:T(8,128)(2,1)S(1)}, bf16[4,2,128,1024]{2,3,1,0:T(8,128)(2,1)S(1)}, u32[]{:S(2)}, u32[]{:S(2)}) collective-permute-start(bf16[4,2,128,1024]{2,3,1,0:T(8,128)(2,1)S(1)} %pad_maximum_fusion.1), channel_id=1, source_target_pairs={{8,0},{10,2},{12,4},{14,6},{16,8},{18,10},{20,12},{22,14},{24,16},... | collective-permute-start | bytes 6291464 | tf_op jit(solution)/shard_map/ppermute | solution.py:16
  245.4 62.4 %all-to-all-start = ((bf16[8,2,128,1024]{2,3,1,0:T(8,128)(2,1)}), bf16[8,2,128,1024]{2,3,1,0:T(8,128)(2,1)}, u32[]{:S(2)}, u32[]{:S(2)}) async-start(bf16[8,2,128,1024]{2,3,1,0:T(8,128)(2,1)} %pad_maximum_fusion), calls=%async_computation | async-start | bytes 8388608 | tf_op jit(solution)/shard_map/all_to_all | solution.py:112
  251.2 34.0 %all-gather.2.cloned.1.call-start = ((), (), s32[]{:S(2)}) async-start(), calls=%async_computation.1 | async-start | bytes 1572864 | tf_op jit(solution)/shard_map/all_gather | solution.py:111
  312.4 416.7 %copy-start = (f32[4]{0:T(128)S(1)}, f32[4]{0:T(128)}, u32[]{:S(2)}) copy-start(f32[4]{0:T(128)} %compare_select_fusion) | copy-start | bytes 52
Sparse Core Ops, SparseCore 0:
  253.6 31.5 all-gather.1
where the time goes:
time: 751 us; the launch traced here: 745 us
  matrix products  254 us (34%)
  other arithmetic  221 us (29%)
  waiting for transfers between devices  130 us (17%)
  local copies, waits for them, and re-layouts  103 us (14%)
  starting transfers between devices  14.3 us (2%)
  between operations  14.1 us (2%)
  loops' own time  8.19 us (1%)
    reduce_sum x32, other arithmetic, accumulate(): cross_real = (own_part[0][:, :, None, :] * partner_part[0][:, None, :, :]...  146 us
    dot_general x32, matrix products, accumulate(): jnp.dot(cross_block, lag_table, preferred_element_type=jnp.float32)  116 us
    ppermute x3, waiting for transfers between devices, from_behind(): return lax.ppermute(x, axis, pairs)  77.8 us
    convert_element_type x32, local copies, waits for them, and re-layouts, accumulate(): cross_block = jnp.stack([cross_real, cross_imag], axis=2).astype(jnp.bflo...  75.7 us
    dot_general x8, matrix products, transform(): lax.dot_general(flat_rows, sine_table, (((1,), (1,)), ((), ())), preferre...  74.8 us
    dot_general x8, matrix products, transform(): lax.dot_general(flat_rows, cosine, (((1,), (1,)), ((), ())), preferred_el...  63.3 us
    all_gather x1, waiting for transfers between devices, per_device(): own_whole = lax.all_gather(whitened, 'freq', axis=2, tiled=True)  31.8 us
    convert_element_type x32, other arithmetic, accumulate(): lax.dynamic_slice_in_dim(partner_split, first, block_width, 3)  30.3 us
  transfers between devices with their start and end apart: 5, of which 5 were waited for; matrix products, arithmetic and copies ran while one was open for 1% of the time, Pallas kernels for 0%

commit v1 on v0

v1 whole, which is shorter than its diff:
```python
import functools
import math

import jax
import jax.numpy as jnp
import ml_dtypes
import numpy as np
from jax import lax
from jax.experimental import pallas as pl
from jax.experimental.pallas import tpu as pltpu
from jax.sharding import PartitionSpec as P

BAND = 64
OFF = 8
LAGS = 128
VMEM_LIMIT = 56 * 1024 * 1024


def leak_spectrum(freqs, samples, window, shift, slots, period):
    steps = np.arange(window)
    tone = np.exp(2j * np.pi * ((freqs[:, None] * (steps - shift)[None]) % samples) / samples)
    bins = np.exp(-2j * np.pi * ((steps[:, None] * slots[None]) % period) / period)
    return tone @ bins


@functools.lru_cache(maxsize=None)
def build_tables(samples):
    width = LAGS
    residues = samples // width
    groups = residues // 2
    half = width // 2
    per_band = BAND // residues
    order = np.concatenate([np.arange(i, half, per_band) for i in range(per_band)])
    steps = np.arange(width)
    slots = np.arange(width + 1)
    forward = np.zeros((groups, 2 * width, 4 * half))
    to_bins = np.zeros((2, groups, 4 * half, 4, width))
    root = 1.0 / math.sqrt(2.0)
    re_a, im_a, re_b, im_b = (slice(i * half, (i + 1) * half) for i in range(4))
    for g in range(groups):
        freq_a = g + residues * order
        freq_b = (residues - g if g else groups) + residues * order
        wave_a = np.exp(-2j * np.pi * ((steps[:, None] * freq_a[None]) % samples) / samples)
        wave_b = np.exp(-2j * np.pi * ((steps[:, None] * freq_b[None]) % samples) / samples)
        top, low = forward[g, :width], forward[g, width:]
        top[:, re_a], top[:, im_a] = wave_a.real, wave_a.imag
        if g == 0:
            low[:, re_b], low[:, im_b] = wave_b.real, wave_b.imag
        else:
            low[:, re_a], low[:, im_a] = -wave_a.imag, wave_a.real
            top[:, re_b], top[:, im_b] = wave_b.real, wave_b.imag
            low[:, re_b], low[:, im_b] = wave_b.imag, -wave_b.real
        for side in range(2):
            window, shift = ((width, 0), (2 * width, half))[side]
            leak = functools.partial(
                leak_spectrum, samples=samples, window=window, shift=shift, slots=slots, period=2 * width
            )
            pos_a, neg_a, pos_b, neg_b = leak(freq_a), leak(-freq_a), leak(freq_b), leak(-freq_b)
            spec = np.zeros((2, 4 * half, width + 1), complex)
            if g == 0:
                zero = (freq_a == 0)[:, None]
                spec[0, re_a] = np.where(zero, pos_a, root * (pos_a + neg_a))
                spec[0, im_a] = np.where(zero, 0.0, root * 1j * (pos_a - neg_a))
                spec[1, re_b] = root * (pos_b + neg_b)
                spec[1, im_b] = root * 1j * (pos_b - neg_b)
            else:
                spec[0, re_a], spec[0, im_a] = root * pos_a, root * 1j * pos_a
                spec[0, re_b], spec[0, im_b] = root * neg_b, -root * 1j * neg_b
                spec[1, re_b], spec[1, im_b] = root * pos_b, root * 1j * pos_b
                spec[1, re_a], spec[1, im_a] = root * neg_a, -root * 1j * neg_a
            table = to_bins[side, g]
            table[:, 0], table[:, 1] = spec[0, :, :width].real, spec[0, :, :width].imag
            table[:, 2], table[:, 3] = spec[1, :, :width].real, spec[1, :, :width].imag
            if g == 0:
                ends = (spec[0, :, 0].real, spec[1, :, 0].real, spec[0, :, width].real, spec[1, :, width].real)
            else:
                ends = tuple(
                    math.sqrt(2.0) * v
                    for v in (spec[0, :, 0].real, spec[0, :, 0].imag, spec[0, :, width].real, spec[0, :, width].imag)
                )
            for q in range(4):
                table[:, q, 0] = ends[q]
    lags = np.arange(LAGS)
    phase = 2 * np.pi * ((steps[:, None] * lags[None]) % (2 * width)) / (2 * width)
    lag = np.stack([2 * np.cos(phase), -2 * np.sin(phase)])
    lag[0, 0], lag[1, 0] = 1.0, (-1.0) ** lags
    bf16 = ml_dtypes.bfloat16
    forward_t = forward.transpose(0, 2, 1)
    forward_hi = forward_t.astype(bf16)
    forward_lo = (forward_t - forward_hi.astype(np.float64)).astype(bf16)
    bins_t = to_bins.transpose(0, 1, 3, 4, 2).reshape(2, groups, 4 * width, 4 * half).astype(bf16)
    lag_t = lag.reshape(2 * width, LAGS).T.astype(bf16)
    scale = residues / (2.0 * width * samples) / math.sqrt(samples)
    return forward_hi, forward_lo, bins_t, lag_t, scale


def real_dft(values):
    n = len(values)
    if n == 2:
        return [(values[0] + values[1], None), (values[0] - values[1], None)]
    even, odd = real_dft(values[0::2]), real_dft(values[1::2])
    out = [None] * (n // 2 + 1)
    for k in range(n // 4 + 1):
        (er, ei), (pr, pi) = even[k], odd[k]
        angle = -2.0 * math.pi * k / n
        c, s = math.cos(angle), math.sin(angle)
        if k == 0:
            out[0] = (er + pr, None)
            out[n // 2] = (er - pr, None)
            continue
        if 4 * k == n:
            out[k] = (er, -pr)
            continue
        if pi is None:
            tr, ti = pr * c, pr * s
        elif 8 * k == n:
            tr, ti = (pr + pi) * c, (pi - pr) * c
        else:
            tr, ti = pr * c - pi * s, pr * s + pi * c
        if ei is None:
            out[k] = (er + tr, ti)
            out[n // 2 - k] = (er - tr, ti)
        else:
            out[k] = (er + tr, ei + ti)
            out[n // 2 - k] = (er - tr, ti - ei)
    return out


def prepare_kernel(own, first_ref, second_ref, fhi_hbm, flo_hbm, bins_hbm, out_ref,
                   fhi, flo, bins, yhi, ylo, spec, wide, sems):
    windows, channels, samples = first_ref.shape
    width = LAGS
    residues = samples // width
    groups = residues // 2
    rows = 2 * windows * channels
    lanes = 2 * channels
    copies = [
        pltpu.make_async_copy(src, dst, sems.at[i])
        for i, (src, dst) in enumerate(((fhi_hbm, fhi), (flo_hbm, flo), (bins_hbm, bins)))
    ]
    for copy in copies:
        copy.start()

    step = 16
    per_window = channels // step

    def split(value):
        high = value.astype(jnp.bfloat16)
        return high, (value - high.astype(jnp.float32)).astype(jnp.bfloat16)

    def transform(n, carry):
        w, c = n // per_window, n % per_window
        for which, ref in enumerate((first_ref, second_ref)):
            if own and which:
                continue
            block = ref[w, pl.ds(pl.multiple_of(c * step, step), step), :].astype(jnp.float32)
            terms = real_dft([block[:, a * width:(a + 1) * width] for a in range(residues)])
            for g in range(groups):
                if g == 0:
                    parts = (terms[0][0], terms[groups][0])
                else:
                    parts = terms[g]
                for side, part in enumerate(parts):
                    hi, lo = split(part)
                    for copy_to in ((0, 1) if own else (which,)):
                        row = pl.multiple_of(w * lanes + copy_to * channels + c * step, step)
                        yhi[g, pl.ds(row, step), side * width:(side + 1) * width] = hi
                        ylo[g, pl.ds(row, step), side * width:(side + 1) * width] = lo
        return carry

    lax.fori_loop(0, windows * per_window, transform, 0)
    copies[0].wait()
    copies[1].wait()
    nt = (((1,), (1,)), ((), ()))
    bands = (samples // 2) // BAND

    def forward(g, power):
        value = lax.dot_general(fhi[g], yhi[g], nt, preferred_element_type=jnp.float32)
        value += lax.dot_general(flo[g], yhi[g], nt, preferred_element_type=jnp.float32)
        value += lax.dot_general(fhi[g], ylo[g], nt, preferred_element_type=jnp.float32)
        spec[g] = value
        squared = (value * value).reshape(2 * width // bands, bands, rows)
        return power + squared.sum(0)

    power = lax.fori_loop(0, groups, forward, jnp.zeros((bands, rows), jnp.float32))
    gain = 1.0 / jnp.sqrt(power * (1.0 / BAND) + 1e-6)
    copies[2].wait()

    def to_bins(g, carry):
        white = (spec[g].reshape(2 * width // bands, bands, rows) * gain[None]).reshape(2 * width, rows)
        value = jnp.dot(bins[g], white.astype(jnp.bfloat16), preferred_element_type=jnp.float32)
        parts = [value[q * width:(q + 1) * width] for q in range(4)]
        if own:
            left = lax.broadcasted_iota(jnp.int32, (width, rows), 1) % lanes < channels
            ends = lax.broadcasted_iota(jnp.int32, (width, rows), 0) == 0
            turned = [parts[1], -parts[0], parts[3], -parts[2]]
            zero = jnp.zeros_like(parts[0])
            real = [parts[q] if q < 2 else jnp.where(ends, zero, parts[q]) for q in range(4)]
            imag = [jnp.where(ends, zero if q < 2 else parts[q], turned[q]) for q in range(4)]
            parts = [jnp.where(left, real[q], imag[q]) for q in range(4)]
        for q in range(4):
            for w in range(windows):
                start = w * (groups * 4) + g * 4 + q
                wide[pl.ds(start, width, stride=windows * groups * 4), :] = parts[q][:, w * lanes:(w + 1) * lanes]
        return carry

    lax.fori_loop(0, groups, to_bins, 0)
    depth = windows * groups * 4

    def narrow(k, carry):
        block = wide[pl.ds(pl.multiple_of(k * depth, depth), depth), :]
        out_ref[k] = (block.T if own else block).astype(jnp.bfloat16)
        return carry

    lax.fori_loop(0, width, narrow, 0)


def prepare(first, second, tables, own):
    windows, channels, samples = first.shape
    forward_hi, forward_lo, bins_t = tables
    width = LAGS
    groups = samples // width // 2
    rows = 2 * windows * channels
    depth = windows * groups * 4
    lanes = 2 * channels
    shape = (width, lanes, depth) if own else (width, depth, lanes)
    any_spec = pl.BlockSpec(memory_space=pl.ANY)
    vmem_spec = pl.BlockSpec(memory_space=pltpu.VMEM)
    flops = 2 * groups * rows * (3 * 4 * width * width + 8 * width * width)
    return pl.pallas_call(
        functools.partial(prepare_kernel, own),
        out_shape=jax.ShapeDtypeStruct(shape, jnp.bfloat16),
        in_specs=[vmem_spec, vmem_spec, any_spec, any_spec, any_spec],
        out_specs=vmem_spec,
        scratch_shapes=[
            pltpu.VMEM(forward_hi.shape, jnp.bfloat16),
            pltpu.VMEM(forward_lo.shape, jnp.bfloat16),
            pltpu.VMEM(bins_t.shape, jnp.bfloat16),
            pltpu.VMEM((groups, rows, 2 * width), jnp.bfloat16),
            pltpu.VMEM((groups, rows, 2 * width), jnp.bfloat16),
            pltpu.VMEM((groups, 2 * width, rows), jnp.float32),
            pltpu.VMEM((width * depth, lanes), jnp.float32),
            pltpu.SemaphoreType.DMA((3,)),
        ],
        compiler_params=pltpu.CompilerParams(vmem_limit_bytes=VMEM_LIMIT),
        cost_estimate=pl.CostEstimate(flops=flops, bytes_accessed=14 * 2**20, transcendentals=0),
        name="prepare_own" if own else "prepare_partners",
    )(first, second, forward_hi, forward_lo, bins_t)


def stack_kernel(chunks, per_chunk, per_out, own_ref, first_ref, second_ref, lag_ref, keep_ref, out_ref, *cross):
    step = pl.program_id(0)
    width = LAGS
    lanes = first_ref.shape[2]
    channels = lanes // 2

    @pl.when(step < chunks)
    def _():
        def one(n, carry):
            k = step * per_chunk + n
            for side, ref in enumerate((first_ref, second_ref)):
                value = jnp.dot(own_ref[n], ref[n], preferred_element_type=jnp.float32)
                for part in range(2):
                    cross[side][pl.ds(part * width + k, channels, stride=2 * width), :] = (
                        value[part * channels:(part + 1) * channels]
                    )
            return carry

        lax.fori_loop(0, per_chunk, one, 0)

    @pl.when(step >= chunks)
    def _():
        def one(n, carry):
            i = (step - chunks) * per_out + n
            part = pl.ds(pl.multiple_of(i * 2 * width, 2 * width), 2 * width)
            block = jnp.concatenate([ref[part, :].astype(jnp.bfloat16) for ref in cross], axis=1)
            value = jnp.dot(lag_ref[...], block, preferred_element_type=jnp.float32).T
            for o in range(4):
                out_ref[o, n] = value[o * channels:(o + 1) * channels] * keep_ref[o]
            return carry

        lax.fori_loop(0, per_out, one, 0)


def stack(own, first, second, lag_t, keep):
    width, lanes, depth = own.shape
    channels = lanes // 2
    chunks, out_chunks = 4, 8
    per_chunk, per_out = width // chunks, channels // out_chunks
    block = lambda s: (jnp.minimum(s, chunks - 1), 0, 0)
    offsets = 4
    return pl.pallas_call(
        functools.partial(stack_kernel, chunks, per_chunk, per_out),
        grid=(chunks + out_chunks,),
        out_shape=jax.ShapeDtypeStruct((offsets, channels, channels, LAGS), jnp.float32),
        in_specs=[
            pl.BlockSpec((per_chunk, lanes, depth), block),
            pl.BlockSpec((per_chunk, depth, lanes), block),
            pl.BlockSpec((per_chunk, depth, lanes), block),
            pl.BlockSpec(lag_t.shape, lambda s: (0, 0)),
            pl.BlockSpec(memory_space=pltpu.SMEM),
        ],
        out_specs=pl.BlockSpec(
            (offsets, per_out, channels, LAGS), lambda s: (0, jnp.maximum(s - chunks, 0), 0, 0)
        ),
        scratch_shapes=[pltpu.VMEM((channels * 2 * width, lanes), jnp.float32)] * 2,
        compiler_params=pltpu.CompilerParams(
            vmem_limit_bytes=VMEM_LIMIT, dimension_semantics=("arbitrary",)
        ),
        name="stack_lags",
    )(own, first, second, lag_t, keep)


def per_device(traces, live, reach):
    windows, channels, samples = traces.shape
    blocks = lax.axis_size("fibre")
    splits = lax.axis_size("freq")
    owned = OFF // splits
    place = lax.axis_index("freq")
    forward_hi, forward_lo, bins_t, lag_t, scale = build_tables(samples)
    forward_hi, forward_lo = jnp.asarray(forward_hi), jnp.asarray(forward_lo)
    masked = traces * live.astype(traces.dtype)[None, :, None]

    def arrive(offset):
        pairs = []
        for b in range(blocks):
            for g in range(splits):
                source = b + g * owned + offset
                if source < blocks:
                    pairs.append((source * splits + g, b * splits + g))
        return lax.ppermute(masked, ("fibre", "freq"), pairs)

    own = prepare(masked, masked, (forward_hi, forward_lo, jnp.asarray(bins_t[1])), True)
    partners = [arrive(k) for k in range(owned)]
    partner_tables = (forward_hi, forward_lo, jnp.asarray(bins_t[0]))
    first = prepare(partners[0], partners[1], partner_tables, False)
    second = prepare(partners[2], partners[3], partner_tables, False)
    offset_ids = place * owned + jnp.arange(owned, dtype=jnp.int32)
    keep = jnp.where(offset_ids < reach[0], jnp.float32(scale), jnp.float32(0.0))
    return stack(own, first, second, jnp.asarray(lag_t), keep)[None]


def solution(mesh):
    placed = (P(None, "fibre", None), P("fibre"), P("fibre"))
    return jax.shard_map(
        per_device,
        mesh=mesh,
        in_specs=placed,
        out_specs=P("fibre", "freq", None, None, None),
        check_vma=False,
    )
```

time: 751 us -> 229 us (0.30)
  matrix products: 254 us -> 0 us
  other arithmetic: 221 us -> 2.51 us
  Pallas kernels: 0 us -> 125 us
  local copies, waits for them, and re-layouts: 103 us -> 0.98 us
  waiting for transfers between devices: 130 us -> 87.6 us
  between operations: 14.1 us -> 0.73 us
  loops' own time: 8.19 us -> 0 us
    dot_general x48 -> x0, matrix products: 254 us -> none  [the longest x32 116 us: accumulate(): jnp.dot(cross_block, lag_table, preferred_element_type=jnp.float32)]
    reduce_sum x33 -> x0, other arithmetic: 146 us -> none  [the longest x32 146 us: accumulate(): cross_real = (own_part[0][:, :, None, :] * partner_part[0][:, None, :, :]...]
    pallas_call x0 -> x4, Pallas kernels: none -> 125 us  [the longest x3 71.5 us: prepare(): pl.pallas_call(functools.partial(prepare_kernel, own), out_shape=jax.Shap...]
    convert_element_type x32 -> x0, local copies, waits for them, and re-layouts: 75.7 us -> none  [accumulate(): cross_block = jnp.stack([cross_real, cross_imag], axis=2).astype(jnp.bflo...]
    convert_element_type x67 -> x1, other arithmetic: 50.8 us -> 0.66 us  [per_device(): masked = traces * live.astype(traces.dtype)[None, :, None]]
    all_gather x1 -> x0, waiting for transfers between devices: 31.8 us -> none  [per_device(): own_whole = lax.all_gather(whitened, 'freq', axis=2, tiled=True)]
    all_to_all x1 -> x0, waiting for transfers between devices: 20.3 us -> none  [per_device(): lax.all_to_all(partners, 'freq', split_axis=0, concat_axis=3, tiled=True)]
    dynamic_slice x16 -> x0, local copies, waits for them, and re-layouts: 12.5 us -> none  [the longest x8 7.3 us: per_device(): lax.map(lambda partner: correlate(own_whole, partner, 0, windows, channel...]
  transfers between devices with their start and end apart: 5 -> 4, of which waited for: 5 -> 3; matrix products, arithmetic and copies ran while one was open for 1% -> 0% of each run, Pallas kernels for 0% -> 23%
where the time goes in v1:
time: 229 us; the launch traced here: 225 us
  Pallas kernels  125 us (55%)
  waiting for transfers between devices  87.6 us (38%)
  starting transfers between devices  8.02 us (4%)
  other arithmetic  2.51 us (1%)
    ppermute x4, waiting for transfers between devices, arrive(): return lax.ppermute(masked, ('fibre', 'freq'), pairs)  87.6 us
    pallas_call x3, Pallas kernels, prepare(): pl.pallas_call(functools.partial(prepare_kernel, own), out_shape=jax.Shap...  71.5 us
    pallas_call x1, Pallas kernels, stack(): pl.pallas_call(functools.partial(stack_kernel, chunks, per_chunk, per_out...  53.5 us
    ppermute x4, starting transfers between devices, arrive(): return lax.ppermute(masked, ('fibre', 'freq'), pairs)  8.02 us
  transfers between devices with their start and end apart: 4, of which 3 were waited for; matrix products, arithmetic and copies ran while one was open for 0% of the time, Pallas kernels for 23%

profile of v1, /device:TPU:21, one launch (start us, length us, event | category | flops | bytes accessed | tf_op | source)
XLA Modules:
  0.0 224.8 jit_solution(18403015530670096633)
XLA Ops:
  0.0 0.7 convert_element_type.3
  0.7 1.4 broadcast_multiply_fusion.first_ref.second_ref
  2.0 0.0 copy-start
  2.0 2.6 %collective-permute-start.1 = (bf16[2,64,4096]{2,1,0:T(8,128)(2,1)S(1)}, bf16[2,64,4096]{2,1,0:T(8,128)(2,1)}, u32[]{:S(2)}, u32[]{:S(2)}) collective-permute-start(bf16[2,64,4096]{2,1,0:T(8,128)(2,1)S(1)} %broadcast_multiply_fusion.first_ref.second_ref), channel_id=1, source_target_pairs={{2,0},{11,1},{4,2},{13,3},{6,4},{15,5},{8,6},{17,7},{10,8},{19,9},... | collective-permute-start | bytes 3145736 | tf_op jit(solution)/shard_map/ppermute | solution.py:331
  4.7 2.1 collective-permute-start
  6.8 1.4 collective-permute-start.3
  8.2 1.9 collective-permute-start.2
  10.7 0.5 compare_select_fusion.keep_ref
  11.2 0.0 copy-done
  11.2 31.6 %prepare_own.1.own_ref = bf16[128,128,128]{2,1,0:T(8,128)(2,1)} custom-call(bf16[2,64,4096]{2,1,0:T(8,128)(2,1)} %copy-done, bf16[2,64,4096]{2,1,0:T(8,128)(2,1)} %copy-done, bf16[16,256,256]{2,1,0:T(8,128)(2,1)} %constant.20.clone.fhi_hbm, bf16[16,256,256]{2,1,0:T(8,128)(2,1)} %constant.21.clone.flo_hbm, bf16[16,512,256]{2,1,0:T(8,128)(2,1)} %constant.22.clone.bins_hbm), custom_call_target="tpu_custom_call" | custom-call | flops 2684354560 | bytes 14680064 | tf_op jit(solution)/shard_map/prepare_own/pallas_call | solution.py:230
  42.9 0.0 collective-permute-done.1.second_ref
  42.9 62.6 %collective-permute-done.first_ref = bf16[2,64,4096]{2,1,0:T(8,128)(2,1)} collective-permute-done((bf16[2,64,4096]{2,1,0:T(8,128)(2,1)S(1)}, bf16[2,64,4096]{2,1,0:T(8,128)(2,1)}, u32[]{:S(2)}, u32[]{:S(2)}) %collective-permute-start) | collective-permute-done | bytes 1048608 | tf_op jit(solution)/shard_map/ppermute | solution.py:331
  105.5 19.9 %prepare_partners.2.first_ref = bf16[128,128,128]{2,1,0:T(8,128)(2,1)} custom-call(bf16[2,64,4096]{2,1,0:T(8,128)(2,1)} %collective-permute-done.first_ref, bf16[2,64,4096]{2,1,0:T(8,128)(2,1)} %collective-permute-done.1.second_ref, bf16[16,256,256]{2,1,0:T(8,128)(2,1)} %constant.20.clone.fhi_hbm, bf16[16,256,256]{2,1,0:T(8,128)(2,1)} %constant.21.clone.flo_hbm, ...), custom_call_target="tpu_custom_call" | custom-call | flops 2684354560 | bytes 14680064 | tf_op jit(solution)/shard_map/prepare_partners/pallas_call | solution.py:230
  125.4 2.5 %collective-permute-done.3.second_ref = bf16[2,64,4096]{2,1,0:T(8,128)(2,1)S(1)} collective-permute-done((bf16[2,64,4096]{2,1,0:T(8,128)(2,1)S(1)}, bf16[2,64,4096]{2,1,0:T(8,128)(2,1)S(1)}, u32[]{:S(2)}, u32[]{:S(2)}) %collective-permute-start.3) | collective-permute-done | bytes 1048608 | tf_op jit(solution)/shard_map/ppermute | solution.py:331
  128.0 0.0 copy-start.1
  128.0 22.5 %collective-permute-done.2.first_ref = bf16[2,64,4096]{2,1,0:T(8,128)(2,1)S(1)} collective-permute-done((bf16[2,64,4096]{2,1,0:T(8,128)(2,1)S(1)}, bf16[2,64,4096]{2,1,0:T(8,128)(2,1)S(1)}, u32[]{:S(2)}, u32[]{:S(2)}) %collective-permute-start.2) | collective-permute-done | bytes 1048608 | tf_op jit(solution)/shard_map/ppermute | solution.py:331
  150.4 0.0 copy-done.1
  150.4 0.0 copy-start.2
  150.4 1.0 copy-done.2
  151.4 19.9 %prepare_partners.3.second_ref = bf16[128,128,128]{2,1,0:T(8,128)(2,1)} custom-call(bf16[2,64,4096]{2,1,0:T(8,128)(2,1)} %copy-done.2, bf16[2,64,4096]{2,1,0:T(8,128)(2,1)} %copy-done.1, bf16[16,256,256]{2,1,0:T(8,128)(2,1)} %constant.20.clone.fhi_hbm, bf16[16,256,256]{2,1,0:T(8,128)(2,1)} %constant.21.clone.flo_hbm, ...), custom_call_target="tpu_custom_call" | custom-call | flops 2684354560 | bytes 14680064 | tf_op jit(solution)/shard_map/prepare_partners/pallas_call | solution.py:230
  171.3 53.5 %stack_lags.1 = f32[4,64,64,128]{3,2,1,0:T(8,128)} custom-call(bf16[128,128,128]{2,1,0:T(8,128)(2,1)} %prepare_own.1.own_ref, bf16[128,128,128]{2,1,0:T(8,128)(2,1)} %prepare_partners.2.first_ref, bf16[128,128,128]{2,1,0:T(8,128)(2,1)} %prepare_partners.3.second_ref, bf16[128,256]{1,0:T(8,128)(2,1)} %constant.24.clone.lag_ref, f32[4]{0:T(128)} %compare_select_fusion.keep_ref), custom_call_target="tpu_custom_call" | custom-call | tf_op jit(solution)/shard_map/stack_lags/pallas_call | solution.py:292
Async XLA Ops:
  2.0 9.2 %copy-start = (bf16[2,64,4096]{2,1,0:T(8,128)(2,1)}, bf16[2,64,4096]{2,1,0:T(8,128)(2,1)S(1)}, u32[]{:S(2)}) copy-start(bf16[2,64,4096]{2,1,0:T(8,128)(2,1)S(1)} %broadcast_multiply_fusion.first_ref.second_ref) | copy-start | bytes 3145732
  2.0 40.8 %collective-permute-start.1 = (bf16[2,64,4096]{2,1,0:T(8,128)(2,1)S(1)}, bf16[2,64,4096]{2,1,0:T(8,128)(2,1)}, u32[]{:S(2)}, u32[]{:S(2)}) collective-permute-start(bf16[2,64,4096]{2,1,0:T(8,128)(2,1)S(1)} %broadcast_multiply_fusion.first_ref.second_ref), channel_id=1, source_target_pairs={{2,0},{11,1},{4,2},{13,3},{6,4},{15,5},{8,6},{17,7},{10,8},{19,9},... | collective-permute-start | bytes 3145736 | tf_op jit(solution)/shard_map/ppermute | solution.py:331
  4.7 100.8 %collective-permute-start = (bf16[2,64,4096]{2,1,0:T(8,128)(2,1)S(1)}, bf16[2,64,4096]{2,1,0:T(8,128)(2,1)}, u32[]{:S(2)}, u32[]{:S(2)}) collective-permute-start(bf16[2,64,4096]{2,1,0:T(8,128)(2,1)S(1)} %broadcast_multiply_fusion.first_ref.second_ref), channel_id=1, source_target_pairs={{0,0},{9,1},{2,2},{11,3},{4,4},{13,5},{6,6},{15,7},{8,8},{17,9},{1... | collective-permute-start | bytes 3145736 | tf_op jit(solution)/shard_map/ppermute | solution.py:331
  6.8 121.2 %collective-permute-start.3 = (bf16[2,64,4096]{2,1,0:T(8,128)(2,1)S(1)}, bf16[2,64,4096]{2,1,0:T(8,128)(2,1)S(1)}, u32[]{:S(2)}, u32[]{:S(2)}) collective-permute-start(bf16[2,64,4096]{2,1,0:T(8,128)(2,1)S(1)} %broadcast_multiply_fusion.first_ref.second_ref), channel_id=1, source_target_pairs={{6,0},{15,1},{8,2},{17,3},{10,4},{19,5},{12,6},{21,7},{14,8},{23,9... | collective-permute-start | bytes 3145736 | tf_op jit(solution)/shard_map/ppermute | solution.py:331
  8.2 142.3 %collective-permute-start.2 = (bf16[2,64,4096]{2,1,0:T(8,128)(2,1)S(1)}, bf16[2,64,4096]{2,1,0:T(8,128)(2,1)S(1)}, u32[]{:S(2)}, u32[]{:S(2)}) collective-permute-start(bf16[2,64,4096]{2,1,0:T(8,128)(2,1)S(1)} %broadcast_multiply_fusion.first_ref.second_ref), channel_id=1, source_target_pairs={{4,0},{13,1},{6,2},{15,3},{8,4},{17,5},{10,6},{19,7},{12,8},{21,9}... | collective-permute-start | bytes 3145736 | tf_op jit(solution)/shard_map/ppermute | solution.py:331
  128.0 22.5 %copy-start.1 = (bf16[2,64,4096]{2,1,0:T(8,128)(2,1)}, bf16[2,64,4096]{2,1,0:T(8,128)(2,1)S(1)}, u32[]{:S(2)}) copy-start(bf16[2,64,4096]{2,1,0:T(8,128)(2,1)S(1)} %collective-permute-done.3.second_ref) | copy-start | bytes 3145732
  150.4 1.0 copy-start.2
